TPU v7x, 1024 devices: a whole 4x4x32 slice. The times are simulated.
1024 devices in a mesh: dom: 64 (over z, core), sub: 16 (over y, x).
Axes of the slice: x: 4, y: 4, z: 32, core: 2. Of those that a mesh axis runs over, the one named last changes fastest.
Arguments:
- a_tiles: bfloat16 [4096, 10, 128, 128], P(('dom', 'sub')), may hold values from -0.5 to 0.5
- a_cols: int32 [4096, 10], P(('dom', 'sub')), may hold values from 0 to 4095, as said below
- a_count: int32 [4096], P(('dom', 'sub')), may hold values from 3 to 10, as said below
- p_tiles: bfloat16 [4096, 128, 256], P(('dom', 'sub')), may hold values from -0.5 to 0.5
- p_cols: int32 [4096, 2], P(('dom', 'sub')), may hold values from 0 to 511, as said below
Outputs:
- coarse_band: bfloat16 [65536, 3072], P(('dom', 'sub'))
Inputs may be any that keep to these rules, and one draw needn't show every extreme that they name: `a_cols`: slot 0 of fine tile f holds f itself. Every column tile of fine tile f lies in its group g(f), or among the last 4 tiles of group g(f) - 1, or among the first 4 tiles of group g(f) + 1. Values in slots at or beyond a_count are such tiles too. `a_count`: each device has at least one fine row tile with all 10 slots live. `p_cols`: both coarse tiles of fine tile f lie in group g(f), between g(f) * 8 and (g(f) + 1) * 8 - 1. With j = f mod 64, the first, h, is within 1 of g(f) * 8 + (j * 8) // 64; the second is g(f) * 8 + (h - g(f) * 8 + 8 // 2) mod 8.
All inputs are finite; a program needn't handle non-finite values.
Results may differ from a plain program's by a relative error of at most 0.0049.
Values may be sent and summed in bfloat16 or wider, within the bound.
A program may use at most 128 MiB of HBM per device.

v0:
```python
import jax
import jax.numpy as jnp
from jax import lax
from jax.sharding import PartitionSpec as P

COARSE_ROWS = 64


def from_behind(value, axis, steps):
    count = lax.axis_size(axis)
    initial, last = (max(0, -steps), min(count, count - steps))
    return lax.ppermute(value, axis, [(source, source + steps) for source in range(initial, last)])


def local(a_tiles, a_cols, a_count, p_tiles, p_cols):
    row_tiles = a_tiles.shape[0]
    slot_count = a_tiles.shape[1]
    tile_size = a_tiles.shape[2]
    sub_count = lax.axis_size("sub")
    group_here = lax.axis_index("dom")
    group_tiles = row_tiles * sub_count
    coarse_group = sub_count * COARSE_ROWS // tile_size
    band_blocks = 3 * coarse_group
    group_p, group_c = (
        lax.all_gather(p_tiles, "sub", axis=0, tiled=True),
        lax.all_gather(p_cols, "sub", axis=0, tiled=True),
    )
    left_p, left_c = from_behind(
        (group_p[group_tiles - row_tiles :], group_c[group_tiles - row_tiles :]), "dom", 1
    )
    right_p, right_c = from_behind((group_p[:row_tiles], group_c[:row_tiles]), "dom", -1)
    pool_p = jnp.concatenate([left_p, group_p, right_p], axis=0)
    pool_c = jnp.concatenate([left_c, group_c, right_c], axis=0)
    first_tile = group_here * group_tiles - row_tiles
    band_base = (group_here - 1) * coarse_group
    block_ids = jnp.arange(band_blocks, dtype=jnp.int32)
    slot_ids = jnp.arange(slot_count, dtype=jnp.int32)

    def row_product(row_inputs):
        a_row, column_ids, live_count = row_inputs
        local_index = column_ids - first_tile
        fetched = jnp.take(pool_p, local_index, axis=0)
        fetched_blocks = jnp.take(pool_c, local_index, axis=0) - band_base
        products = jnp.einsum("kab,kbc->kac", a_row, fetched, preferred_element_type=jnp.float32)
        live_slots = (slot_ids < live_count).astype(jnp.float32)
        selector = (fetched_blocks[:, :, None] == block_ids[None, None, :]).astype(
            jnp.float32
        ) * live_slots[:, None, None]
        split_products = products.reshape(slot_count, tile_size, 2, tile_size)
        q_block = jnp.einsum(
            "katb,ktc->acb", split_products, selector, precision=lax.Precision.HIGHEST
        )
        return q_block.reshape(tile_size, band_blocks * tile_size).astype(jnp.bfloat16)

    q_all = lax.map(row_product, (a_tiles, a_cols, a_count))
    q_flat = q_all.reshape(row_tiles * tile_size, band_blocks * tile_size)
    coarse_ids = jnp.arange(coarse_group, dtype=jnp.int32)
    home_blocks = p_cols - group_here * coarse_group
    placing = (home_blocks[:, :, None] == coarse_ids[None, None, :]).astype(jnp.bfloat16)
    split_p = p_tiles.reshape(row_tiles, tile_size, 2, tile_size)
    placed = jnp.einsum(
        "fatb,ftn->fanb", split_p, placing, preferred_element_type=jnp.float32
    ).astype(jnp.bfloat16)
    placed = placed.reshape(row_tiles * tile_size, coarse_group * tile_size)
    owned = lax.psum_scatter(
        lax.dot_general(
            placed, q_flat, (((0,), (0,)), ((), ())), preferred_element_type=jnp.float32
        ),
        "sub",
        scatter_dimension=0,
        tiled=True,
    )
    return owned.astype(jnp.bfloat16)


def solution(mesh):
    placed = (
        P(("dom", "sub"), None, None, None),
        P(("dom", "sub"), None),
        P(("dom", "sub")),
        P(("dom", "sub"), None, None),
        P(("dom", "sub"), None),
    )
    return jax.shard_map(
        local, mesh=mesh, in_specs=placed, out_specs=P(("dom", "sub"), None), check_vma=False
    )
```

profile of v0, /device:TPU:1, one launch (start us, length us, event | category | flops | bytes accessed | tf_op | source)
XLA Modules:
  0.0 314.7 jit_solution(8441172902166771023)
XLA Ops:
  6.5 0.7 all-gather.3.cloned.1.call-update
  7.3 0.0 reduce-scatter.2.cloned.1.call-start
  7.3 19.1 %all-gather = s32[16,4,2]{1,2,0:T(2,128)S(1)} all-gather(s32[1,4,2]{1,2,0:T(2,128)} %bitcast.58), channel_id=1, replica_groups=mesh['dom'=64,'sub'=16] {'sub'}, dimensions={0}, use_global_device_ids=true | all-gather | bytes 544 | tf_op jit(solution)/shard_map/all_gather | solution.py:26
  26.4 9.5 %collective-permute-start = (s32[4,2]{0,1:T(2,128)S(1)}, s32[4,2]{0,1:T(2,128)S(1)}, u32[]{:S(2)}, u32[]{:S(2)}) collective-permute-start(s32[4,2]{0,1:T(2,128)S(1)} %get-tuple-element.140), channel_id=1, source_target_pairs={{0,16},{16,32},{32,48},{48,64},{64,80},{80,96},{96,112},{112,128},... | collective-permute-start | bytes 104 | tf_op jit(solution)/shard_map/ppermute | solution.py:12
  35.8 8.8 %collective-permute-start.1 = (s32[4,2]{0,1:T(2,128)S(1)}, s32[4,2]{0,1:T(2,128)S(1)}, u32[]{:S(2)}, u32[]{:S(2)}) collective-permute-start(s32[4,2]{0,1:T(2,128)S(1)} %get-tuple-element.141), channel_id=1, source_target_pairs={{16,0},{32,16},{48,32},{64,48},{80,64},{96,80},{112,96},{128,112},... | collective-permute-start | bytes 104 | tf_op jit(solution)/shard_map/ppermute | solution.py:12
  44.7 1.0 reshape.76
  45.7 0.7 broadcast_subtract_fusion
  46.4 0.1 copy.23
  46.5 0.1 reshape.96
  46.6 60.7 %all-gather.3.cloned.1.call-done = bf16[64,128,256]{2,1,0:T(8,128)(2,1)} async-done(((bf16[4,128,256]{2,1,0:T(8,128)(2,1)}), bf16[64,128,256]{2,1,0:T(8,128)(2,1)}) %all-gather.3.cloned.1.call-update) | async-done | bytes 4194320 | tf_op jit(solution)/shard_map/all_gather | solution.py:25
  107.3 1.1 fusion.34
  108.4 3.7 %collective-permute-start.2 = (bf16[4,128,256]{2,1,0:T(8,128)(2,1)S(1)}, bf16[4,128,256]{2,1,0:T(8,128)(2,1)S(1)}, u32[]{:S(2)}, u32[]{:S(2)}) collective-permute-start(bf16[4,128,256]{2,1,0:T(8,128)(2,1)S(1)} %get-tuple-element.138), channel_id=1, source_target_pairs={{0,16},{16,32},{32,48},{48,64},{64,80},{80,96},{96,112},{112,128},... | collective-permute-start | bytes 786440 | tf_op jit(solution)/shard_map/ppermute | solution.py:12
  112.1 1.9 collective-permute-start.3
  114.1 1.6 convolution_convert_fusion
  115.6 0.1 pad_add_fusion
  115.7 0.1 copy.25
  115.8 0.0 copy-start.1
  115.8 4.0 %collective-permute-done.3 = bf16[4,128,256]{2,1,0:T(8,128)(2,1)S(1)} collective-permute-done((bf16[4,128,256]{2,1,0:T(8,128)(2,1)S(1)}, bf16[4,128,256]{2,1,0:T(8,128)(2,1)S(1)}, u32[]{:S(2)}, u32[]{:S(2)}) %collective-permute-start.3) | collective-permute-done | bytes 262176 | tf_op jit(solution)/shard_map/ppermute | solution.py:12
  119.8 4.1 %pad_maximum_fusion = bf16[72,128,256]{2,1,0:T(8,128)(2,1)} fusion(bf16[4,128,256]{2,1,0:T(8,128)(2,1)S(1)} %collective-permute-done.3, bf16[64,128,256]{2,1,0:T(8,128)(2,1)} %all-gather.3.cloned.1.call-done, bf16[4,128,256]{2,1,0:T(8,128)(2,1)S(1)} %collective-permute-done.2), kind=kLoop, calls=%fused_computation.33 | loop fusion | flops 4718592 | bytes 9437184 | tf_op jit(solution)/shard_map/concatenate | solution.py:32
  123.9 41.8 %while.11 = (s32[]{:T(128)}, bf16[4,128,3072]{2,1,0:T(8,128)(2,1)}, s32[4,10]{1,0:T(4,128)S(1)}, s32[]{:T(128)}, s32[72,2]{1,0:T(8,128)S(1)}, /*index=5*/s32[]{:...) while((s32[]{:T(128)}, bf16[4,128,3072]{2,1,0:T(8,128)(2,1)}, ...), condition=%wide.region_1.2_spmd.clone, body=%wide.region_0.1_spmd.clone.sunk | while | flops 178980960 | bytes 11473959 | solution.py:55
  123.9 0.6 dynamic_slice.33
  124.5 0.6 compare_convert_fusion.2
  125.2 0.6 gather_fusion.1
  125.8 0.1 copy.42
  125.9 2.9 gather_fusion
  128.8 1.4 fusion.49
  130.2 0.7 reshape.117
  130.9 2.2 fusion.50
  133.1 0.3 convert_element_type.51
  133.4 1.0 constant_dynamic-update-slice_fusion.2
  134.4 0.6 dynamic_slice.33
  135.0 0.6 compare_convert_fusion.2
  135.7 0.6 gather_fusion.1
  136.2 0.1 copy.42
  136.3 2.9 gather_fusion
  139.3 1.4 fusion.49
  140.7 0.7 reshape.117
  141.3 2.2 fusion.50
  143.6 0.3 convert_element_type.51
  143.9 0.9 constant_dynamic-update-slice_fusion.2
  144.8 0.6 dynamic_slice.33
  145.4 0.6 compare_convert_fusion.2
  146.1 0.6 gather_fusion.1
  146.7 0.1 copy.42
  146.8 2.9 gather_fusion
  149.7 1.4 fusion.49
  151.1 0.7 reshape.117
  151.8 2.2 fusion.50
  154.0 0.3 convert_element_type.51
  154.3 1.0 constant_dynamic-update-slice_fusion.2
  155.3 0.6 dynamic_slice.33
  155.9 0.6 compare_convert_fusion.2
  156.6 0.6 gather_fusion.1
  157.1 0.1 copy.42
  157.2 2.9 gather_fusion
  160.2 1.4 fusion.49
  161.5 0.7 reshape.117
  162.2 2.2 fusion.50
  164.4 0.3 convert_element_type.51
  164.8 1.0 constant_dynamic-update-slice_fusion.2
  165.7 10.2 %fusion.27 = f32[1024,3072]{1,0:T(8,128)} fusion(bf16[512,3072]{1,0:T(8,128)(2,1)} %bitcast.59, bf16[64,8,8,128]{3,2,1,0:T(8,128)(2,1)} %bitcast.57), kind=kOutput, calls=%fused_computation.35 | convolution fusion | flops 3221225472 | bytes 16777216 | tf_op jit(solution)/shard_map/dot_general | solution.py:66
  175.9 0.0 reduce-scatter.2.cloned.1.call-update
  176.0 130.0 %reduce-scatter.2.cloned.1.call-done = f32[64,3072]{1,0:T(8,128)} async-done(((f32[1024,3072]{1,0:T(8,128)}), f32[64,3072]{1,0:T(8,128)}) %reduce-scatter.2.cloned.1.call-update) | async-done | bytes 786448 | tf_op jit(solution)/shard_map/reduce_scatter | solution.py:65
  305.9 1.9 convert_element_type.36
  (26 shorter events, 0.2 us)
Async XLA Ops:
  6.5 100.8 %all-gather.3.cloned.1.call-start = ((), (), s32[]{:S(2)}) async-start(), calls=%async_computation.1 | async-start | bytes 4456448 | tf_op jit(solution)/shard_map/all_gather | solution.py:25
  7.3 298.7 %reduce-scatter.2.cloned.1.call-start = ((), (), s32[]{:S(2)}) async-start(), calls=%async_computation.2 | async-start | bytes 13369344 | tf_op jit(solution)/shard_map/reduce_scatter | solution.py:65
  26.4 89.2 %collective-permute-start = (s32[4,2]{0,1:T(2,128)S(1)}, s32[4,2]{0,1:T(2,128)S(1)}, u32[]{:S(2)}, u32[]{:S(2)}) collective-permute-start(s32[4,2]{0,1:T(2,128)S(1)} %get-tuple-element.140), channel_id=1, source_target_pairs={{0,16},{16,32},{32,48},{48,64},{64,80},{80,96},{96,112},{112,128},... | collective-permute-start | bytes 104 | tf_op jit(solution)/shard_map/ppermute | solution.py:12
  35.8 79.8 %collective-permute-start.1 = (s32[4,2]{0,1:T(2,128)S(1)}, s32[4,2]{0,1:T(2,128)S(1)}, u32[]{:S(2)}, u32[]{:S(2)}) collective-permute-start(s32[4,2]{0,1:T(2,128)S(1)} %get-tuple-element.141), channel_id=1, source_target_pairs={{16,0},{32,16},{48,32},{64,48},{80,64},{96,80},{112,96},{128,112},... | collective-permute-start | bytes 104 | tf_op jit(solution)/shard_map/ppermute | solution.py:12
  108.4 7.4 %collective-permute-start.2 = (bf16[4,128,256]{2,1,0:T(8,128)(2,1)S(1)}, bf16[4,128,256]{2,1,0:T(8,128)(2,1)S(1)}, u32[]{:S(2)}, u32[]{:S(2)}) collective-permute-start(bf16[4,128,256]{2,1,0:T(8,128)(2,1)S(1)} %get-tuple-element.138), channel_id=1, source_target_pairs={{0,16},{16,32},{32,48},{48,64},{64,80},{80,96},{96,112},{112,128},... | collective-permute-start | bytes 786440 | tf_op jit(solution)/shard_map/ppermute | solution.py:12
  112.1 7.7 %collective-permute-start.3 = (bf16[4,128,256]{2,1,0:T(8,128)(2,1)S(1)}, bf16[4,128,256]{2,1,0:T(8,128)(2,1)S(1)}, u32[]{:S(2)}, u32[]{:S(2)}) collective-permute-start(bf16[4,128,256]{2,1,0:T(8,128)(2,1)S(1)} %get-tuple-element.139), channel_id=1, source_target_pairs={{16,0},{32,16},{48,32},{64,48},{80,64},{96,80},{112,96},{128,112},... | collective-permute-start | bytes 786440 | tf_op jit(solution)/shard_map/ppermute | solution.py:12
  115.8 8.1 %copy-start = (s32[4,10]{1,0:T(4,128)S(1)}, s32[4,10]{1,0:T(4,128)}, u32[]{:S(2)}) copy-start(s32[4,10]{1,0:T(4,128)} %param.8) | copy-start | bytes 484
  115.8 8.1 %copy-start.1 = (s32[4]{0:T(128)S(1)}, s32[4]{0:T(128)}, u32[]{:S(2)}) copy-start(s32[4]{0:T(128)} %param.9) | copy-start | bytes 52
Sparse Core Ops, SparseCore 0:
  11.5 95.7 all-gather.2
  176.1 129.8 reduce-scatter.1
where the time goes:
time: 315 us
  waiting for transfers between devices  195 us (62%)
  local copies, waits for them, and re-layouts  26.9 us (9%)
  matrix products  26.1 us (8%)
  starting transfers between devices  24 us (8%)
  blocking collectives  19.1 us (6%)
  between operations  13.5 us (4%)
  other arithmetic  9.43 us (3%)
    reduce_scatter x1, waiting for transfers between devices, local(): lax.psum_scatter(lax.dot_general(placed, q_flat, (((0,), (0,)), ((), ()))...  130 us
    all_gather x1, waiting for transfers between devices, local(): lax.all_gather(p_tiles, 'sub', axis=0, tiled=True)  60.7 us
    ppermute x4, starting transfers between devices, from_behind(): lax.ppermute(value, axis, [(source, source + steps) for source in range(i...  23.9 us
    all_gather x1, blocking collectives, local(): lax.all_gather(p_cols, 'sub', axis=0, tiled=True)  19.1 us
    gather x4, local copies, waits for them, and re-layouts, row_product(): fetched = jnp.take(pool_p, local_index, axis=0)  11.7 us
    dot_general x1, matrix products, local(): lax.dot_general(placed, q_flat, (((0,), (0,)), ((), ())), preferred_eleme...  10.2 us
    dot_general x4, matrix products, row_product(): jnp.einsum('katb,ktc->acb', split_products, selector, precision=lax.Preci...  8.81 us
  transfers between devices with their start and end apart: 6, of which 3 were waited for; matrix products, arithmetic and copies ran while one was open for 1% of the time, Pallas kernels for 0%

commit v1 on v0

v1 whole, which is shorter than its diff:
```python
import jax
import jax.numpy as jnp
from jax import lax
from jax.experimental import pallas as pl
from jax.experimental.pallas import tpu as pltpu
from jax.sharding import PartitionSpec as P

MESH = pl.DeviceIdType.MESH

AXES = 4
CUBE = 16
LEFT, RIGHT = CUBE, CUBE + 1
GATHER = [(step, 0 if piece == 0 else 2 ** (piece - 1), 1 if piece == 0 else 2 ** (piece - 1))
          for step in range(AXES) for piece in range(step + 1)]
BASE = [0, 8, 12, 14]
REDUCE = [(step, BASE[step] + (0 if piece == 0 else 2 ** (piece - 1)), 1 if piece == 0 else 2 ** (piece - 1))
          for step in range(AXES) for piece in reversed(range(AXES - step))]


def cube_bits(x, y):
    return [(x + x // 2) % 2, (y + y // 2) % 2, x // 2, y // 2]


def rotated(rel, part):
    power = (1 + part % 2) * (1 + 3 * (part // 2))
    return rel // power + (rel % power) * (CUBE // power)


def kernel(a_hbm, cols, count, p_ref, pcols, out_ref, pool, meta, a_ref, prod, pair_of, q, pt, keep, sent, got,
           a_sem, ag_send, ag_recv, meta_send, meta_recv, halo_send, halo_recv, rs_send, rs_recv):
    f_tiles, slots, tile = a_ref.shape[0], a_ref.shape[1], a_ref.shape[2]
    unit = keep.shape[2]
    width = keep.shape[3]
    dom, sub = lax.axis_index("dom"), lax.axis_index("sub")
    doms = lax.axis_size("dom")
    x, y = lax.rem(sub, 4), lax.div(sub, 4)
    bits = cube_bits(x, y)
    xa, xb = x + 1 - 2 * (x % 2), 3 - x
    ya, yb = y + 1 - 2 * (y % 2), 3 - y

    def partner(axis):
        in_x, high = (axis + 1) % 2, axis // 2
        px = in_x * ((1 - high) * xa + high * xb) + (1 - in_x) * x
        py = (1 - in_x) * ((1 - high) * ya + high * yb) + in_x * y
        return (dom, py * 4 + px)

    after = (lax.rem(dom + 1, doms), sub)
    before = (lax.rem(dom + doms - 1, doms), sub)

    barrier = pltpu.get_barrier_semaphore()
    for other in [partner(axis) for axis in range(AXES)] + [after, before]:
        pl.semaphore_signal(barrier, inc=1, device_id=other, device_id_type=MESH)

    a_copy = pltpu.make_async_copy(a_hbm, a_ref, a_sem)
    a_copy.start()

    def arrange(i, carry):
        high = (pcols[i, 0] - dom * 8) // 4
        first = p_ref[i, :, :tile].astype(jnp.float32)
        second = p_ref[i, :, tile:].astype(jnp.float32)
        swap = jnp.full(first.shape, high, jnp.int32) != 0
        pool[i, 0, :, :tile] = jnp.where(swap, second, first).astype(jnp.bfloat16)
        pool[i, 0, :, tile:] = jnp.where(swap, first, second).astype(jnp.bfloat16)
        meta[0, i] = jnp.full(meta.shape[2:], pcols[i, 0] % 4, jnp.int32)
        return carry

    lax.fori_loop(0, f_tiles, arrange, 0)
    pl.semaphore_wait(barrier, 6)

    def gather_copy(i, at):
        step, first, number = GATHER[at]
        return pltpu.make_async_remote_copy(
            src_ref=pool.at[i, pl.ds(first, number)],
            dst_ref=pool.at[i, pl.ds(first + 2 ** step, number)],
            send_sem=ag_send.at[i, at],
            recv_sem=ag_recv.at[i, at],
            device_id=partner((i + step) % AXES),
            device_id_type=MESH,
        )

    def meta_copy(at):
        step, first, number = GATHER[at]
        return pltpu.make_async_remote_copy(
            src_ref=meta.at[pl.ds(first, number)],
            dst_ref=meta.at[pl.ds(first + 2 ** step, number)],
            send_sem=meta_send.at[at],
            recv_sem=meta_recv.at[at],
            device_id=partner(step),
            device_id_type=MESH,
        )

    for at, (step, first, number) in enumerate(GATHER):
        if first == 0:
            meta_copy(at).start()

            def send_own(i, carry, at=at):
                gather_copy(i, at).start()
                return carry

            lax.fori_loop(0, AXES, send_own, 0)

    for f in range(f_tiles):
        turned = pool[f, 0].astype(jnp.float32).T
        pair = jnp.full(turned.shape, pcols[f, 0] % 4, jnp.int32)
        for r in range(AXES):
            pt[r, :, f * tile:(f + 1) * tile] = jnp.where(pair == r, turned, 0.0).astype(jnp.bfloat16)

    for step in range(AXES):
        arrived = [at for at in range(len(GATHER)) if GATHER[at][0] == step]
        onward = [at for at in range(len(GATHER)) if GATHER[at][0] > step and GATHER[at][1] == 2 ** step]
        for at in arrived:
            meta_copy(at).wait_recv()
        for at in onward:
            meta_copy(at).start()

        def pass_on(i, carry, arrived=arrived, onward=onward):
            for at in arrived:
                gather_copy(i, at).wait_recv()
            for at in onward:
                gather_copy(i, at).start()
            return carry

        lax.fori_loop(0, AXES, pass_on, 0)

    def away(source):
        theirs = cube_bits(source % 4, source // 4)
        return sum(((bits[axis] + theirs[axis]) % 2) * 2 ** axis for axis in range(AXES))

    last, head = away(CUBE - 1), away(0)

    def halo_copy(i, side):
        rel, other = ((last, after), (head, before))[side]
        return pltpu.make_async_remote_copy(
            src_ref=pool.at[i, rotated(rel, i)],
            dst_ref=pool.at[i, CUBE + side],
            send_sem=halo_send.at[side, i],
            recv_sem=halo_recv.at[side, i],
            device_id=other,
            device_id_type=MESH,
        )

    def halo_meta(side):
        rel, other = ((last, after), (head, before))[side]
        return pltpu.make_async_remote_copy(
            src_ref=meta.at[rel],
            dst_ref=meta.at[CUBE + side],
            send_sem=halo_send.at[side, f_tiles],
            recv_sem=halo_recv.at[side, f_tiles],
            device_id=other,
            device_id_type=MESH,
        )

    for side in range(2):
        halo_meta(side).start()

    def halo_start(i, carry):
        for side in range(2):
            halo_copy(i, side).start()
        return carry

    lax.fori_loop(0, f_tiles, halo_start, 0)
    a_copy.wait()
    for side in range(2):
        halo_meta(side).wait_recv()

    def halo_wait(i, carry):
        for side in range(2):
            halo_copy(i, side).wait_recv()
        return carry

    lax.fori_loop(0, f_tiles, halo_wait, 0)

    def place(column):
        u = column - dom * (CUBE * f_tiles) + f_tiles
        part, at = u % f_tiles, u // f_tiles
        source = (at + CUBE - 1) % CUBE
        rel = away(source)
        turned = [rotated(rel, i) for i in range(AXES)]
        slot = jnp.where(part == 0, turned[0], jnp.where(part == 1, turned[1], jnp.where(part == 2, turned[2], turned[3])))
        is_left, is_right = at == 0, at == CUBE + 1
        slot = jnp.where(is_left, LEFT, jnp.where(is_right, RIGHT, slot))
        rel = jnp.where(is_left, LEFT, jnp.where(is_right, RIGHT, rel))
        offset = jnp.where(is_left, -2, jnp.where(is_right, 6, 2))
        return part, slot, rel, offset

    def multiply(f, carry):
        def one(k, carry):
            part, slot, rel, offset = place(cols[f, k])
            product = jnp.dot(a_ref[f, k], pool[part, slot], preferred_element_type=jnp.float32)
            for half in range(2):
                prod[f, k, half] = product[:, half * tile:(half + 1) * tile].reshape(prod.shape[3:])
            offset = jnp.where(k < count[f], offset, -100)
            pair_of[f, k] = meta[rel, part] + offset
            return carry

        return lax.fori_loop(0, slots, one, carry)

    lax.fori_loop(0, f_tiles, multiply, 0)

    def reduce_copy(i, at):
        step, first, number = REDUCE[at]
        return pltpu.make_async_remote_copy(
            src_ref=sent.at[i, pl.ds(first if step == 0 else first + 8, number)],
            dst_ref=got.at[i, pl.ds(first, number)],
            send_sem=rs_send.at[i, at],
            recv_sem=rs_recv.at[i, at],
            device_id=partner((i + AXES - 1 - step) % AXES),
            device_id_type=MESH,
        )

    def start_reduce(i, step):
        for at in range(len(REDUCE)):
            if REDUCE[at][0] == step:
                reduce_copy(i, at).start()

    def terms(i, carry):
        def add_up(f, carry):
            for j in range(2):
                for half in range(2):
                    total = jnp.zeros(prod.shape[3:], jnp.float32)
                    for k in range(slots):
                        live = (pair_of[f, k] == 2 * i + j).astype(jnp.float32)
                        total = total + prod[f, k, half] * live[None]
                    rows = pl.ds(pl.multiple_of(f * tile, tile), tile)
                    q[2 * i + j, rows, half * tile:(half + 1) * tile] = total.reshape(tile, tile).astype(jnp.bfloat16)
            return carry

        lax.fori_loop(0, f_tiles, add_up, 0)
        for j in range(2):
            columns = slice(j * 2 * tile, (j + 1) * 2 * tile)
            for r in range(AXES):
                block = jnp.dot(pt[r], q[2 * i + j], preferred_element_type=jnp.float32)
                for at in range(4):
                    upper, half = at // 2, at % 2
                    slot = rotated(away(2 * r + half + 8 * upper), i)
                    rows = block[upper * tile + half * unit:upper * tile + (half + 1) * unit]
                    keep[i, slot, :, columns] = rows
                    sent[i, (slot + 8) % CUBE, :, columns] = rows.astype(jnp.bfloat16)
        start_reduce(i, 0)
        return carry

    lax.fori_loop(0, AXES, terms, 0)

    def total_of(i, low, step):
        number = max(low, 1)
        for at, (earlier, first, _) in enumerate(REDUCE):
            if earlier < step and first == BASE[earlier] + low:
                reduce_copy(i, at).wait_recv()
        value = keep[i, low:low + number]
        for earlier in range(step):
            value = value + got[i, BASE[earlier] + low:BASE[earlier] + low + number].astype(jnp.float32)
        return value.astype(jnp.bfloat16)

    for step in range(1, AXES):
        low = 2 ** (AXES - 1 - step)

        def send_on(i, carry, step=step, low=low):
            sent[i, BASE[step] + 8:BASE[step] + 8 + low] = total_of(i, low, step)
            start_reduce(i, step)
            return carry

        lax.fori_loop(0, AXES, send_on, 0)

    empty = jnp.zeros((unit, 2 * tile), jnp.bfloat16)
    for block in (0, 4, 18, 22):
        out_ref[:, block * tile:(block + 2) * tile] = empty
    for i in range(AXES):
        mine = total_of(i, 0, AXES)[0]
        for j in range(2):
            pair = 2 * i + j
            block = pair + 2 if pair < 2 else (pair + 6 if pair < 6 else pair + 10)
            for half in range(2):
                columns = slice((block + 4 * half) * tile, (block + 4 * half + 1) * tile)
                out_ref[:, columns] = mine[:, (2 * j + half) * tile:(2 * j + half + 1) * tile]

    def sent_off(i, carry):
        for at in range(len(GATHER)):
            gather_copy(i, at).wait_send()
        for at in range(len(REDUCE)):
            reduce_copy(i, at).wait_send()
        for side in range(2):
            halo_copy(i, side).wait_send()
        return carry

    lax.fori_loop(0, AXES, sent_off, 0)
    for at in range(len(GATHER)):
        meta_copy(at).wait_send()
    for side in range(2):
        halo_meta(side).wait_send()


def local(a_tiles, a_cols, a_count, p_tiles, p_cols):
    f_tiles, slots, tile, _ = a_tiles.shape
    unit = 64
    vmem, smem = pl.BlockSpec(memory_space=pltpu.VMEM), pl.BlockSpec(memory_space=pltpu.SMEM)
    dma = pltpu.SemaphoreType.DMA
    return pl.pallas_call(
        kernel,
        out_shape=jax.ShapeDtypeStruct((unit, 24 * tile), jnp.bfloat16),
        in_specs=[pl.BlockSpec(memory_space=pl.ANY), smem, smem, vmem, smem],
        out_specs=vmem,
        scratch_shapes=[
            pltpu.VMEM((f_tiles, CUBE + 2, tile, 2 * tile), jnp.bfloat16),
            pltpu.VMEM((CUBE + 2, f_tiles, 8, tile), jnp.int32),
            pltpu.VMEM((f_tiles, slots, tile, tile), jnp.bfloat16),
            pltpu.VMEM((f_tiles, slots, 2, tile // 8, 8, tile), jnp.float32),
            pltpu.VMEM((f_tiles, slots, 8, tile), jnp.int32),
            pltpu.VMEM((8, f_tiles * tile, 2 * tile), jnp.bfloat16),
            pltpu.VMEM((AXES, 2 * tile, f_tiles * tile), jnp.bfloat16),
            pltpu.VMEM((AXES, CUBE, unit, 4 * tile), jnp.float32),
            pltpu.VMEM((AXES, CUBE + 7, unit, 4 * tile), jnp.bfloat16),
            pltpu.VMEM((AXES, 15, unit, 4 * tile), jnp.bfloat16),
            dma,
            dma((AXES, len(GATHER))),
            dma((AXES, len(GATHER))),
            dma((len(GATHER),)),
            dma((len(GATHER),)),
            dma((2, f_tiles + 1)),
            dma((2, f_tiles + 1)),
            dma((AXES, len(REDUCE))),
            dma((AXES, len(REDUCE))),
        ],
        compiler_params=pltpu.CompilerParams(collective_id=0, has_side_effects=True, vmem_limit_bytes=48 * 2 ** 20),
    )(a_tiles, a_cols, a_count, p_tiles, p_cols)


def solution(mesh):
    placed = (
        P(("dom", "sub"), None, None, None),
        P(("dom", "sub"), None),
        P(("dom", "sub")),
        P(("dom", "sub"), None, None),
        P(("dom", "sub"), None),
    )
    return jax.shard_map(
        local, mesh=mesh, in_specs=placed, out_specs=P(("dom", "sub"), None), check_vma=False
    )
```

time: 315 us -> 93.8 us (0.30)
  the two profiles are of different devices: /device:TPU:1 before, /device:TPU:16 now
where the time goes in v1:
time: 93.8 us; the launch traced here: 93.6 us
  Pallas kernels  88.5 us (94%)
  local copies, waits for them, and re-layouts  5.11 us (5%)
    pallas_call x1, Pallas kernels, local(): pl.pallas_call(kernel, out_shape=jax.ShapeDtypeStruct((unit, 24 * tile),...  88.5 us
    unnamed x10, local copies, waits for them, and re-layouts  5.11 us

profile of v1, /device:TPU:16, one launch (start us, length us, event | category | flops | bytes accessed | tf_op | source)
XLA Modules:
  0.0 93.6 jit_solution(3174063250536926321)
XLA Ops:
  0.0 0.8 copy.6.pcols
  0.8 0.0 copy-start
  0.8 1.3 %copy-done = bf16[4,10,128,128]{3,2,1,0:T(8,128)(2,1)S(1)} copy-done((bf16[4,10,128,128]{3,2,1,0:T(8,128)(2,1)S(1)}, bf16[4,10,128,128]{3,2,1,0:T(8,128)(2,1)}, u32[]{:S(2)}) %copy-start) | copy-done | bytes 1310744
  2.1 0.0 copy-start.1
  2.1 0.9 %copy-done.1 = bf16[4,128,256]{2,1,0:T(8,128)(2,1)S(1)} copy-done((bf16[4,128,256]{2,1,0:T(8,128)(2,1)S(1)}, bf16[4,128,256]{2,1,0:T(8,128)(2,1)}, u32[]{:S(2)}) %copy-start.1) | copy-done | bytes 262168
  3.0 0.0 copy-start.2
  3.0 0.7 copy-done.2
  3.7 0.0 copy-start.3
  3.7 0.7 copy-done.3
  4.4 88.5 %shard_map.55 = bf16[64,3072]{1,0:T(8,128)(2,1)S(1)} custom-call(bf16[4,10,128,128]{3,2,1,0:T(8,128)(2,1)S(1)} %copy-done, s32[4,10]{1,0:T(4,128)S(1)} %copy-done.2, s32[4]{0:T(128)S(1)} %copy-done.3, bf16[4,128,256]{2,1,0:T(8,128)(2,1)S(1)} %copy-done.1, s32[4,2]{1,0:T(4,128)S(1)} %copy.6.pcols), custom_call_target="tpu_custom_call" | custom-call | tf_op jit(solution)/shard_map/pallas_call | solution.py:297
  92.8 0.7 copy.8
Async XLA Ops:
  0.8 1.3 %copy-start = (bf16[4,10,128,128]{3,2,1,0:T(8,128)(2,1)S(1)}, bf16[4,10,128,128]{3,2,1,0:T(8,128)(2,1)}, u32[]{:S(2)}) copy-start(bf16[4,10,128,128]{3,2,1,0:T(8,128)(2,1)} %a_hbm.1) | copy-start | bytes 3932164
  2.1 0.9 %copy-start.1 = (bf16[4,128,256]{2,1,0:T(8,128)(2,1)S(1)}, bf16[4,128,256]{2,1,0:T(8,128)(2,1)}, u32[]{:S(2)}) copy-start(bf16[4,128,256]{2,1,0:T(8,128)(2,1)} %p_ref.1) | copy-start | bytes 786436
  3.0 0.7 copy-start.2
  3.7 0.7 copy-start.3

commit v2 on v1

v2 whole, which is shorter than its diff:
```python
import jax
import jax.numpy as jnp
from jax import lax
from jax.experimental import pallas as pl
from jax.experimental.pallas import tpu as pltpu
from jax.sharding import PartitionSpec as P

MESH = pl.DeviceIdType.MESH

AXES = 4
CUBE = 16
LEFT, RIGHT = CUBE, CUBE + 1
GATHER = [(0, 0), (0, 1), (0, 2), (1, 1), (0, 3), (1, 2), (2, 2), (3, 2), (1, 3), (2, 3), (3, 3),
          (4, 3), (5, 3), (6, 3), (7, 3)]
GATHER_DEPTH = 3
BASE = [0, 8, 12, 14]
REDUCE = [(0, 6, 2), (0, 4, 2), (1, 10, 2), (0, 2, 2), (1, 9, 1), (0, 1, 1), (2, 13, 1), (1, 8, 1), (0, 0, 1),
          (2, 12, 1), (3, 14, 1)]
REDUCE_DEPTH = 2


def cube_bits(x, y):
    return [(x + x // 2) % 2, (y + y // 2) % 2, x // 2, y // 2]


def rotated(rel, part):
    power = (1 + part % 2) * (1 + 3 * (part // 2))
    return rel // power + (rel % power) * (CUBE // power)


def kernel(a_hbm, cols, count, p_hbm, pcols, out_ref, pool, meta, a_ref, p_ref, turned, pt, prod, q, keep, leaf, sent, got,
           meta_s, where_s, prev_s, last_s,
           a_sem, p_sem, s_sem, ag_send, ag_recv, meta_send, meta_recv, halo_send, halo_recv, rs_send, rs_recv):
    f_tiles, slots, tile = a_ref.shape[0], a_ref.shape[1], a_ref.shape[2]
    unit = keep.shape[2]
    dom, sub = lax.axis_index("dom"), lax.axis_index("sub")
    doms = lax.axis_size("dom")
    x, y = sub % 4, sub // 4
    bits = cube_bits(x, y)
    xa, xb = x + 1 - 2 * (x % 2), 3 - x
    ya, yb = y + 1 - 2 * (y % 2), 3 - y

    def partner(axis):
        in_x, high = (axis + 1) % 2, axis // 2
        px = in_x * ((1 - high) * xa + high * xb) + (1 - in_x) * x
        py = (1 - in_x) * ((1 - high) * ya + high * yb) + in_x * y
        return (dom, py * 4 + px)

    def away(source):
        theirs = cube_bits(source % 4, source // 4)
        return sum(((bits[axis] + theirs[axis]) % 2) * 2 ** axis for axis in range(AXES))

    after = (lax.rem(dom + 1, doms), sub)
    before = (lax.rem(dom + doms - 1, doms), sub)

    p_copy = pltpu.make_async_copy(p_hbm, p_ref, p_sem)
    p_copy.start()
    barrier = pltpu.get_barrier_semaphore()
    for other in [partner(axis) for axis in range(AXES)] + [after, before]:
        pl.semaphore_signal(barrier, inc=1, device_id=other, device_id_type=MESH)
    a_copy = pltpu.make_async_copy(a_hbm, a_ref, a_sem)
    a_copy.start()

    lanes = lax.broadcasted_iota(jnp.int32, meta.shape[1:], 1)
    meta[0] = sum(jnp.where(lanes == f, pcols[0, f] % 4, 0) for f in range(f_tiles))
    p_copy.wait()

    def arrange(i, carry):
        high = (pcols[0, i] - dom * 8) // 4
        first = p_ref[i, :, :tile].astype(jnp.float32)
        second = p_ref[i, :, tile:].astype(jnp.float32)
        swap = jnp.full(first.shape, high, jnp.int32) != 0
        pool[i, 0, :, :tile] = jnp.where(swap, second, first).astype(jnp.bfloat16)
        pool[i, 0, :, tile:] = jnp.where(swap, first, second).astype(jnp.bfloat16)
        return carry

    lax.fori_loop(0, f_tiles, arrange, 0)
    pl.semaphore_wait(barrier, 6)

    last, head = away(CUBE - 1), away(0)

    def final_slot(i, at):
        ahead, behind = rotated(last, i), rotated(head, i)
        begin = jnp.where(ahead // 4 == 1, ahead % 4, jnp.where(behind // 4 == 1, behind % 4, 0))
        return 4 + (at - (len(GATHER) - 4) + begin) % 4

    def gather_copy(i, at):
        slot, step = GATHER[at]
        if slot >= 4:
            slot = final_slot(i, at)
        landing = slot + 2 ** step
        return pltpu.make_async_remote_copy(
            src_ref=pool.at[i, slot],
            dst_ref=pool.at[i, landing],
            send_sem=ag_send.at[i, at],
            recv_sem=ag_recv.at[i, landing],
            device_id=partner((i + step) % AXES),
            device_id_type=MESH,
        )

    def arrival(i, slot):
        return pltpu.make_async_copy(pool.at[i, slot], pool.at[i, slot], ag_recv.at[i, slot])

    def meta_copy(step):
        return pltpu.make_async_remote_copy(
            src_ref=meta.at[pl.ds(0, 2 ** step)],
            dst_ref=meta.at[pl.ds(2 ** step, 2 ** step)],
            send_sem=meta_send.at[step],
            recv_sem=meta_recv.at[step],
            device_id=partner(step),
            device_id_type=MESH,
        )

    def halo_copy(i, side):
        rel, other = ((last, after), (head, before))[side]
        return pltpu.make_async_remote_copy(
            src_ref=pool.at[i, rotated(rel, i)],
            dst_ref=pool.at[i, CUBE + side],
            send_sem=halo_send.at[side, i],
            recv_sem=halo_recv.at[side, i],
            device_id=other,
            device_id_type=MESH,
        )

    def halo_meta(side):
        rel, other = ((last, after), (head, before))[side]
        return pltpu.make_async_remote_copy(
            src_ref=meta.at[rel],
            dst_ref=meta.at[CUBE + side],
            send_sem=halo_send.at[side, f_tiles],
            recv_sem=halo_recv.at[side, f_tiles],
            device_id=other,
            device_id_type=MESH,
        )

    def place(f, carry):
        for k in range(slots):
            u = cols[f, k] - dom * (CUBE * f_tiles) + f_tiles
            part, at = u % f_tiles, u // f_tiles
            rel = away((at + CUBE - 1) % CUBE)
            turns = [rotated(rel, i) for i in range(AXES)]
            slot = jnp.where(part == 0, turns[0], jnp.where(part == 1, turns[1], jnp.where(part == 2, turns[2], turns[3])))
            is_left, is_right = at == 0, at == CUBE + 1
            where_s[0, f * slots + k] = part
            where_s[1, f * slots + k] = jnp.where(is_left, LEFT, jnp.where(is_right, RIGHT, slot))
            where_s[2, f * slots + k] = jnp.where(is_left, LEFT, jnp.where(is_right, RIGHT, rel))
            where_s[3, f * slots + k] = jnp.where(is_left, -2, jnp.where(is_right, 6, 2))
        return carry

    def turn(f, carry):
        turned[f] = pool[f, 0].astype(jnp.float32).T
        return carry

    def lay_out(i, carry):
        for f in range(f_tiles):
            pair = jnp.full((unit, tile), pcols[0, f] % 4, jnp.int32)
            for owner in range(CUBE):
                rows = slice((owner // 8) * tile + (owner % 2) * unit, (owner // 8) * tile + (owner % 2 + 1) * unit)
                slot = rotated(away(owner), i)
                value = jnp.where(pair == (owner // 2) % 4, turned[f, rows], 0.0).astype(jnp.bfloat16)
                pt[i, slot, :, f * tile:(f + 1) * tile] = value
        return carry

    def chain(f, carry):
        pairs = []
        for k in range(slots):
            at = f * slots + k
            pair = meta_s[where_s[2, at], 0, where_s[0, at]] + where_s[3, at]
            pairs.append(jnp.where(k < count[f], pair, -1))
        for k in range(slots):
            found = slots
            for earlier in range(k):
                found = jnp.where(pairs[earlier] == pairs[k], earlier, found)
            prev_s[f * slots + k] = jnp.int32(found)
        for pair in range(8):
            found = slots
            for k in range(slots):
                found = jnp.where(pairs[k] == pair, k, found)
            last_s[f * 8 + pair] = found
        return carry

    meta_copy(0).start()
    seen = {0}
    for at, (slot, step) in enumerate(GATHER):
        new = slot if slot not in seen else None
        seen.add(slot)

        def send(i, carry, at=at, new=new):
            if new is not None:
                arrival(i, new).wait()
            if at >= GATHER_DEPTH:
                gather_copy(i, at - GATHER_DEPTH).wait_send()
            gather_copy(i, at).start()
            return carry

        if slot == 4:
            def early(i, carry):
                for late in range(4, 8):
                    arrival(i, late).wait()
                for side, rel in enumerate((last, head)):
                    @pl.when(rotated(rel, i) < 8)
                    def _():
                        halo_copy(i, side).start()
                return carry

            seen.update(range(4, 8))
            lax.fori_loop(0, AXES, early, 0)

            def send(i, carry, at=at):
                gather_copy(i, at - GATHER_DEPTH).wait_send()
                gather_copy(i, at).start()
                return carry

        lax.fori_loop(0, AXES, send, 0)
        if at == 1:
            lax.fori_loop(0, f_tiles, turn, 0)
        if at == 2:
            lax.fori_loop(0, 2, lay_out, 0)
        if at == 3:
            meta_copy(0).wait_recv()
            meta_copy(1).start()
        if at == 4:
            lax.fori_loop(2, AXES, lay_out, 0)
        if at == 5:
            meta_copy(1).wait_recv()
            meta_copy(2).start()
        if at == 6:
            lax.fori_loop(0, f_tiles, place, 0)
        if at == 8:
            meta_copy(2).wait_recv()
            meta_copy(3).start()
        if at == 11:
            meta_copy(3).wait_recv()
            for side in range(2):
                halo_meta(side).start()
        if at == 13:
            for side in range(2):
                halo_meta(side).wait_recv()
            to_scalars = pltpu.make_async_copy(meta, meta_s, s_sem)
            to_scalars.start()
            to_scalars.wait()
            lax.fori_loop(0, f_tiles, chain, 0)

    for f in range(f_tiles):
        prod[f, slots] = jnp.zeros(prod.shape[2:], jnp.float32)

    def late(i, carry):
        for side, rel in enumerate((last, head)):
            mine = rotated(rel, i)

            @pl.when(mine >= 8)
            def _():
                arrival(i, mine).wait()
                halo_copy(i, side).start()
        return carry

    lax.fori_loop(0, AXES, late, 0)

    def rest(i, carry):
        ahead, behind = rotated(last, i), rotated(head, i)
        for slot in range(8, CUBE):
            @pl.when((slot - ahead) * (slot - behind) != 0)
            def _():
                arrival(i, slot).wait()
        return carry

    lax.fori_loop(0, AXES, rest, 0)
    a_copy.wait()

    def halo_wait(i, carry):
        for side in range(2):
            halo_copy(i, side).wait_recv()
        return carry

    lax.fori_loop(0, f_tiles, halo_wait, 0)

    def multiply(f, carry):
        for k in range(slots):
            at = f * slots + k
            product = jnp.dot(a_ref[f, k], pool[where_s[0, at], where_s[1, at]], preferred_element_type=jnp.float32)
            prod[f, k] = product + prod[f, prev_s[at]] if k else product
        return carry

    lax.fori_loop(0, f_tiles, multiply, 0)

    def reduce_copy(i, at):
        step, first, number = REDUCE[at]
        return pltpu.make_async_remote_copy(
            src_ref=leaf.at[i, pl.ds(first, number)] if step == 0 else sent.at[i, pl.ds(first - 8, number)],
            dst_ref=got.at[i, pl.ds(first, number)],
            send_sem=rs_send.at[i, at],
            recv_sem=rs_recv.at[i, at],
            device_id=partner((i + AXES - 1 - step) % AXES),
            device_id_type=MESH,
        )

    def far_terms(i, carry):
        for j in range(2):
            for f in range(f_tiles):
                rows = slice(f * tile, (f + 1) * tile)
                q[2 * i + j, rows] = prod[f, last_s[f * 8 + 2 * i + j]].astype(jnp.bfloat16)
        far = pt[i, 8:].reshape(8 * unit, f_tiles * tile)
        for j in range(2):
            columns = slice(j * 2 * tile, (j + 1) * 2 * tile)
            block = jnp.dot(far, q[2 * i + j], preferred_element_type=jnp.float32)
            leaf[i, :, :, columns] = block.reshape(8, unit, 2 * tile).astype(jnp.bfloat16)
        for at in range(REDUCE_DEPTH):
            reduce_copy(i, at).start()
        return carry

    lax.fori_loop(0, AXES, far_terms, 0)

    def near_terms(i, carry):
        near = pt[i, :8].reshape(8 * unit, f_tiles * tile)
        for j in range(2):
            columns = slice(j * 2 * tile, (j + 1) * 2 * tile)
            block = jnp.dot(near, q[2 * i + j], preferred_element_type=jnp.float32)
            keep[i, :, :, columns] = block.reshape(8, unit, 2 * tile)
        return carry

    lax.fori_loop(0, AXES, near_terms, 0)

    taken = set()

    def waits(step, low, number):
        found = []
        for at, (earlier, first, length) in enumerate(REDUCE):
            begin = first - BASE[earlier]
            if earlier < step and begin < low + number and low < begin + length and at not in taken:
                taken.add(at)
                found.append(at)
        return found

    def total_of(i, step, low, number):
        value = keep[i, low:low + number]
        for earlier in range(step):
            value = value + got[i, BASE[earlier] + low:BASE[earlier] + low + number].astype(jnp.float32)
        return value.astype(jnp.bfloat16)

    for at, (step, first, number) in enumerate(REDUCE):
        if at < REDUCE_DEPTH:
            continue
        low = 2 ** (AXES - 1 - step) + first - BASE[step]
        needed = waits(step, low, number) if step else []

        def send_on(i, carry, at=at, step=step, first=first, number=number, low=low, needed=needed):
            for other in needed:
                reduce_copy(i, other).wait_recv()
            if step:
                sent[i, first - 8:first - 8 + number] = total_of(i, step, low, number)
            reduce_copy(i, at - REDUCE_DEPTH).wait_send()
            reduce_copy(i, at).start()
            return carry

        lax.fori_loop(0, AXES, send_on, 0)

    empty = jnp.zeros((unit, 2 * tile), jnp.bfloat16)
    for block in (0, 4, 18, 22):
        out_ref[:, block * tile:(block + 2) * tile] = empty
    needed = waits(AXES, 0, 1)
    for i in range(AXES):
        for other in needed:
            reduce_copy(i, other).wait_recv()
        mine = total_of(i, AXES, 0, 1)[0]
        for j in range(2):
            pair = 2 * i + j
            block = pair + 2 if pair < 2 else (pair + 6 if pair < 6 else pair + 10)
            for half in range(2):
                columns = slice((block + 4 * half) * tile, (block + 4 * half + 1) * tile)
                out_ref[:, columns] = mine[:, (2 * j + half) * tile:(2 * j + half + 1) * tile]

    def sent_off(i, carry):
        for at in range(len(GATHER) - GATHER_DEPTH, len(GATHER)):
            gather_copy(i, at).wait_send()
        for at in range(len(REDUCE) - REDUCE_DEPTH, len(REDUCE)):
            reduce_copy(i, at).wait_send()
        for side in range(2):
            halo_copy(i, side).wait_send()
        return carry

    lax.fori_loop(0, AXES, sent_off, 0)
    for step in range(AXES):
        meta_copy(step).wait_send()
    for side in range(2):
        halo_meta(side).wait_send()


def local(a_tiles, a_cols, a_count, p_tiles, p_cols):
    f_tiles, slots, tile, _ = a_tiles.shape
    unit = 64
    hbm, smem = pl.BlockSpec(memory_space=pl.ANY), pl.BlockSpec(memory_space=pltpu.SMEM)
    dma = pltpu.SemaphoreType.DMA
    return pl.pallas_call(
        kernel,
        out_shape=jax.ShapeDtypeStruct((unit, 24 * tile), jnp.bfloat16),
        in_specs=[hbm, smem, smem, hbm, smem],
        out_specs=pl.BlockSpec(memory_space=pltpu.VMEM),
        scratch_shapes=[
            pltpu.VMEM((f_tiles, CUBE + 2, tile, 2 * tile), jnp.bfloat16),
            pltpu.VMEM((CUBE + 2, 8, tile), jnp.int32),
            pltpu.VMEM((f_tiles, slots, tile, tile), jnp.bfloat16),
            pltpu.VMEM((f_tiles, tile, 2 * tile), jnp.bfloat16),
            pltpu.VMEM((f_tiles, 2 * tile, tile), jnp.float32),
            pltpu.VMEM((AXES, CUBE, unit, f_tiles * tile), jnp.bfloat16),
            pltpu.VMEM((f_tiles, slots + 1, tile, 2 * tile), jnp.float32),
            pltpu.VMEM((8, f_tiles * tile, 2 * tile), jnp.bfloat16),
            pltpu.VMEM((AXES, 8, unit, 4 * tile), jnp.float32),
            pltpu.VMEM((AXES, 8, unit, 4 * tile), jnp.bfloat16),
            pltpu.VMEM((AXES, 7, unit, 4 * tile), jnp.bfloat16),
            pltpu.VMEM((AXES, 15, unit, 4 * tile), jnp.bfloat16),
            pltpu.SMEM((CUBE + 2, 8, tile), jnp.int32),
            pltpu.SMEM((4, f_tiles * slots), jnp.int32),
            pltpu.SMEM((f_tiles * slots,), jnp.int32),
            pltpu.SMEM((f_tiles * 8,), jnp.int32),
            dma,
            dma,
            dma,
            dma((AXES, len(GATHER))),
            dma((AXES, CUBE)),
            dma((AXES,)),
            dma((AXES,)),
            dma((2, f_tiles + 1)),
            dma((2, f_tiles + 1)),
            dma((AXES, len(REDUCE))),
            dma((AXES, len(REDUCE))),
        ],
        compiler_params=pltpu.CompilerParams(collective_id=0, has_side_effects=True, vmem_limit_bytes=60 * 2 ** 20),
    )(a_tiles, a_cols, a_count, p_tiles, p_cols.T)


def solution(mesh):
    placed = (
        P(("dom", "sub"), None, None, None),
        P(("dom", "sub"), None),
        P(("dom", "sub")),
        P(("dom", "sub"), None, None),
        P(("dom", "sub"), None),
    )
    return jax.shard_map(
        local, mesh=mesh, in_specs=placed, out_specs=P(("dom", "sub"), None), check_vma=False
    )
```

time: 93.8 us -> 75.9 us (0.81)
  the two profiles are of different devices: /device:TPU:16 before, /device:TPU:8 now
where the time goes in v2:
time: 75.9 us; the launch traced here: 75.6 us
  Pallas kernels  73.9 us (97%)
  local copies, waits for them, and re-layouts  1.77 us (2%)
    pallas_call x1, Pallas kernels, local(): pl.pallas_call(kernel, out_shape=jax.ShapeDtypeStruct((unit, 24 * tile),...  73.9 us
    unnamed x1, local copies, waits for them, and re-layouts  1.77 us

profile of v2, /device:TPU:8, one launch (start us, length us, event | category | flops | bytes accessed | tf_op | source)
XLA Modules:
  0.0 75.6 jit_solution(10996350830873383300)
XLA Ops:
  0.0 73.9 %shard_map.55 = bf16[64,3072]{1,0:T(8,128)(2,1)} custom-call(bf16[4,10,128,128]{3,2,1,0:T(8,128)(2,1)} %a_hbm.1, s32[4,10]{1,0:T(4,128)} %cols.1, s32[4]{0:T(128)} %count.1, bf16[4,128,256]{2,1,0:T(8,128)(2,1)} %p_hbm.1, s32[2,4]{1,0:T(2,128)} %bitcast.1), custom_call_target="tpu_custom_call" | custom-call | tf_op jit(solution)/shard_map/pallas_call | solution.py:393
  73.9 1.8 %copy.7 = bf16[64,3072]{1,0:T(8,128)(2,1)} copy(bf16[64,3072]{1,0:T(8,128)(2,1)} %shard_map.55) | data formatting | bytes 786432

commit v3 on v2

--- a/solution.py
+++ b/solution.py
@@ -92,7 +92,7 @@
         return pltpu.make_async_remote_copy(
             src_ref=pool.at[i, slot],
             dst_ref=pool.at[i, landing],
-            send_sem=ag_send.at[i, at],
+            send_sem=ag_send.at[i, at % GATHER_DEPTH],
             recv_sem=ag_recv.at[i, landing],
             device_id=partner((i + step) % AXES),
             device_id_type=MESH,
@@ -116,8 +116,8 @@
         return pltpu.make_async_remote_copy(
             src_ref=pool.at[i, rotated(rel, i)],
             dst_ref=pool.at[i, CUBE + side],
-            send_sem=halo_send.at[side, i],
-            recv_sem=halo_recv.at[side, i],
+            send_sem=halo_send.at[0, side],
+            recv_sem=halo_recv.at[0, side],
             device_id=other,
             device_id_type=MESH,
         )
@@ -127,11 +127,15 @@
         return pltpu.make_async_remote_copy(
             src_ref=meta.at[rel],
             dst_ref=meta.at[CUBE + side],
-            send_sem=halo_send.at[side, f_tiles],
-            recv_sem=halo_recv.at[side, f_tiles],
+            send_sem=halo_send.at[1, side],
+            recv_sem=halo_recv.at[1, side],
             device_id=other,
             device_id_type=MESH,
         )
+
+    def halo_all(side, sems):
+        landed = pool.at[:, CUBE + side]
+        return pltpu.make_async_copy(landed, landed, sems.at[0, side])
 
     def place(f, carry):
         for k in range(slots):
@@ -224,8 +228,6 @@
         if at == 5:
             meta_copy(1).wait_recv()
             meta_copy(2).start()
-        if at == 6:
-            lax.fori_loop(0, f_tiles, place, 0)
         if at == 8:
             meta_copy(2).wait_recv()
             meta_copy(3).start()
@@ -238,9 +240,10 @@
                 halo_meta(side).wait_recv()
             to_scalars = pltpu.make_async_copy(meta, meta_s, s_sem)
             to_scalars.start()
-            to_scalars.wait()
-            lax.fori_loop(0, f_tiles, chain, 0)
-
+
+    lax.fori_loop(0, f_tiles, place, 0)
+    to_scalars.wait()
+    lax.fori_loop(0, f_tiles, chain, 0)
     for f in range(f_tiles):
         prod[f, slots] = jnp.zeros(prod.shape[2:], jnp.float32)
 
@@ -267,12 +270,8 @@
     lax.fori_loop(0, AXES, rest, 0)
     a_copy.wait()
 
-    def halo_wait(i, carry):
-        for side in range(2):
-            halo_copy(i, side).wait_recv()
-        return carry
-
-    lax.fori_loop(0, f_tiles, halo_wait, 0)
+    for side in range(2):
+        halo_all(side, halo_recv).wait()
 
     def multiply(f, carry):
         for k in range(slots):
@@ -288,7 +287,7 @@
         return pltpu.make_async_remote_copy(
             src_ref=leaf.at[i, pl.ds(first, number)] if step == 0 else sent.at[i, pl.ds(first - 8, number)],
             dst_ref=got.at[i, pl.ds(first, number)],
-            send_sem=rs_send.at[i, at],
+            send_sem=rs_send.at[i, at % REDUCE_DEPTH],
             recv_sem=rs_recv.at[i, at],
             device_id=partner((i + AXES - 1 - step) % AXES),
             device_id_type=MESH,
@@ -374,14 +373,13 @@
             gather_copy(i, at).wait_send()
         for at in range(len(REDUCE) - REDUCE_DEPTH, len(REDUCE)):
             reduce_copy(i, at).wait_send()
-        for side in range(2):
-            halo_copy(i, side).wait_send()
         return carry
 
     lax.fori_loop(0, AXES, sent_off, 0)
     for step in range(AXES):
         meta_copy(step).wait_send()
     for side in range(2):
+        halo_all(side, halo_send).wait()
         halo_meta(side).wait_send()
 
 
@@ -415,13 +413,13 @@
             dma,
             dma,
             dma,
-            dma((AXES, len(GATHER))),
+            dma((AXES, GATHER_DEPTH)),
             dma((AXES, CUBE)),
             dma((AXES,)),
             dma((AXES,)),
-            dma((2, f_tiles + 1)),
-            dma((2, f_tiles + 1)),
-            dma((AXES, len(REDUCE))),
+            dma((2, 2)),
+            dma((2, 2)),
+            dma((AXES, REDUCE_DEPTH)),
             dma((AXES, len(REDUCE))),
         ],
         compiler_params=pltpu.CompilerParams(collective_id=0, has_side_effects=True, vmem_limit_bytes=60 * 2 ** 20),

time: 75.9 us -> 74.1 us (0.976)
  Pallas kernels: 73.9 us -> 72.1 us
    pallas_call x1, Pallas kernels: 73.9 us -> 72.1 us  [local(): pl.pallas_call(kernel, out_shape=jax.ShapeDtypeStruct((unit, 24 * tile),...]
where the time goes in v3:
time: 74.1 us; the launch traced here: 73.9 us
  Pallas kernels  72.1 us (97%)
  local copies, waits for them, and re-layouts  1.77 us (2%)
    pallas_call x1, Pallas kernels, local(): pl.pallas_call(kernel, out_shape=jax.ShapeDtypeStruct((unit, 24 * tile),...  72.1 us
    unnamed x1, local copies, waits for them, and re-layouts  1.77 us

profile of v3, /device:TPU:8, one launch (start us, length us, event | category | flops | bytes accessed | tf_op | source)
XLA Modules:
  0.0 73.9 jit_solution(14971880887665543332)
XLA Ops:
  0.0 72.1 %shard_map.55 = bf16[64,3072]{1,0:T(8,128)(2,1)} custom-call(bf16[4,10,128,128]{3,2,1,0:T(8,128)(2,1)} %a_hbm.1, s32[4,10]{1,0:T(4,128)} %cols.1, s32[4]{0:T(128)} %count.1, bf16[4,128,256]{2,1,0:T(8,128)(2,1)} %p_hbm.1, s32[2,4]{1,0:T(2,128)} %bitcast.1), custom_call_target="tpu_custom_call" | custom-call | tf_op jit(solution)/shard_map/pallas_call | solution.py:391
  72.1 1.8 %copy.7 = bf16[64,3072]{1,0:T(8,128)(2,1)} copy(bf16[64,3072]{1,0:T(8,128)(2,1)} %shard_map.55) | data formatting | bytes 786432

commit v4 on v3

--- a/solution.py
+++ b/solution.py
@@ -10,7 +10,7 @@
 AXES = 4
 CUBE = 16
 LEFT, RIGHT = CUBE, CUBE + 1
-GATHER = [(0, 0), (0, 1), (0, 2), (1, 1), (0, 3), (1, 2), (2, 2), (3, 2), (1, 3), (2, 3), (3, 3),
+GATHER = [(0, 0), (0, 1), (0, 2), (0, 3), (1, 1), (1, 2), (2, 2), (3, 2), (1, 3), (2, 3), (3, 3),
           (4, 3), (5, 3), (6, 3), (7, 3)]
 GATHER_DEPTH = 3
 BASE = [0, 8, 12, 14]
@@ -28,9 +28,9 @@
     return rel // power + (rel % power) * (CUBE // power)
 
 
-def kernel(a_hbm, cols, count, p_hbm, pcols, out_ref, pool, meta, a_ref, p_ref, turned, pt, prod, q, keep, leaf, sent, got,
-           meta_s, where_s, prev_s, last_s,
-           a_sem, p_sem, s_sem, ag_send, ag_recv, meta_send, meta_recv, halo_send, halo_recv, rs_send, rs_recv):
+def kernel(a_hbm, cols_hbm, count_hbm, p_hbm, pcols_hbm, out_ref, pool, meta, a_ref, turned, pt, prod, q, keep, leaf, sent, got,
+           cols, count, pcols, meta_s, where_s, prev_s, last_s,
+           scalar_sems, a_sem, p_sem, s_sem, ag_send, ag_recv, meta_send, meta_recv, halo_send, halo_recv, rs_send, rs_recv):
     f_tiles, slots, tile = a_ref.shape[0], a_ref.shape[1], a_ref.shape[2]
     unit = keep.shape[2]
     dom, sub = lax.axis_index("dom"), lax.axis_index("sub")
@@ -53,28 +53,20 @@
     after = (lax.rem(dom + 1, doms), sub)
     before = (lax.rem(dom + doms - 1, doms), sub)
 
-    p_copy = pltpu.make_async_copy(p_hbm, p_ref, p_sem)
+    p_copy = pltpu.make_async_copy(p_hbm, pool.at[:, 0], p_sem)
     p_copy.start()
     barrier = pltpu.get_barrier_semaphore()
     for other in [partner(axis) for axis in range(AXES)] + [after, before]:
         pl.semaphore_signal(barrier, inc=1, device_id=other, device_id_type=MESH)
     a_copy = pltpu.make_async_copy(a_hbm, a_ref, a_sem)
     a_copy.start()
-
-    lanes = lax.broadcasted_iota(jnp.int32, meta.shape[1:], 1)
-    meta[0] = sum(jnp.where(lanes == f, pcols[0, f] % 4, 0) for f in range(f_tiles))
+    scalar_copies = [pltpu.make_async_copy(source, target, scalar_sems.at[at])
+                     for at, (source, target) in enumerate([(pcols_hbm, pcols), (cols_hbm, cols), (count_hbm, count)])]
+    for copy in scalar_copies:
+        copy.start()
+
     p_copy.wait()
 
-    def arrange(i, carry):
-        high = (pcols[0, i] - dom * 8) // 4
-        first = p_ref[i, :, :tile].astype(jnp.float32)
-        second = p_ref[i, :, tile:].astype(jnp.float32)
-        swap = jnp.full(first.shape, high, jnp.int32) != 0
-        pool[i, 0, :, :tile] = jnp.where(swap, second, first).astype(jnp.bfloat16)
-        pool[i, 0, :, tile:] = jnp.where(swap, first, second).astype(jnp.bfloat16)
-        return carry
-
-    lax.fori_loop(0, f_tiles, arrange, 0)
     pl.semaphore_wait(barrier, 6)
 
     last, head = away(CUBE - 1), away(0)
@@ -152,7 +144,10 @@
         return carry
 
     def turn(f, carry):
-        turned[f] = pool[f, 0].astype(jnp.float32).T
+        swap = jnp.full((tile, tile), (pcols[0, f] - dom * 8) // 4, jnp.int32) != 0
+        first, second = (pool[f, 0, :, half * tile:(half + 1) * tile].astype(jnp.float32) for half in range(2))
+        turned[f, :tile] = jnp.where(swap, second, first).T
+        turned[f, tile:] = jnp.where(swap, first, second).T
         return carry
 
     def lay_out(i, carry):
@@ -169,7 +164,9 @@
         pairs = []
         for k in range(slots):
             at = f * slots + k
-            pair = meta_s[where_s[2, at], 0, where_s[0, at]] + where_s[3, at]
+            home = meta_s[where_s[2, at], 0, where_s[0, at]]
+            where_s[4, at] = home // 4
+            pair = home % 4 + where_s[3, at]
             pairs.append(jnp.where(k < count[f], pair, -1))
         for k in range(slots):
             found = slots
@@ -183,7 +180,6 @@
             last_s[f * 8 + pair] = found
         return carry
 
-    meta_copy(0).start()
     seen = {0}
     for at, (slot, step) in enumerate(GATHER):
         new = slot if slot not in seen else None
@@ -217,6 +213,10 @@
 
         lax.fori_loop(0, AXES, send, 0)
         if at == 1:
+            scalar_copies[0].wait()
+            lanes = lax.broadcasted_iota(jnp.int32, meta.shape[1:], 1)
+            meta[0] = sum(jnp.where(lanes == f, pcols[0, f] - dom * 8, 0) for f in range(f_tiles))
+            meta_copy(0).start()
             lax.fori_loop(0, f_tiles, turn, 0)
         if at == 2:
             lax.fori_loop(0, 2, lay_out, 0)
@@ -241,6 +241,8 @@
             to_scalars = pltpu.make_async_copy(meta, meta_s, s_sem)
             to_scalars.start()
 
+    for copy in scalar_copies[1:]:
+        copy.wait()
     lax.fori_loop(0, f_tiles, place, 0)
     to_scalars.wait()
     lax.fori_loop(0, f_tiles, chain, 0)
@@ -277,6 +279,9 @@
         for k in range(slots):
             at = f * slots + k
             product = jnp.dot(a_ref[f, k], pool[where_s[0, at], where_s[1, at]], preferred_element_type=jnp.float32)
+            swap = jnp.full((tile, tile), where_s[4, at], jnp.int32) != 0
+            first, second = product[:, :tile], product[:, tile:]
+            product = jnp.concatenate([jnp.where(swap, second, first), jnp.where(swap, first, second)], axis=1)
             prod[f, k] = product + prod[f, prev_s[at]] if k else product
         return carry
 
@@ -386,18 +391,17 @@
 def local(a_tiles, a_cols, a_count, p_tiles, p_cols):
     f_tiles, slots, tile, _ = a_tiles.shape
     unit = 64
-    hbm, smem = pl.BlockSpec(memory_space=pl.ANY), pl.BlockSpec(memory_space=pltpu.SMEM)
+    hbm = pl.BlockSpec(memory_space=pl.ANY)
     dma = pltpu.SemaphoreType.DMA
     return pl.pallas_call(
         kernel,
         out_shape=jax.ShapeDtypeStruct((unit, 24 * tile), jnp.bfloat16),
-        in_specs=[hbm, smem, smem, hbm, smem],
+        in_specs=[hbm] * 5,
         out_specs=pl.BlockSpec(memory_space=pltpu.VMEM),
         scratch_shapes=[
             pltpu.VMEM((f_tiles, CUBE + 2, tile, 2 * tile), jnp.bfloat16),
             pltpu.VMEM((CUBE + 2, 8, tile), jnp.int32),
             pltpu.VMEM((f_tiles, slots, tile, tile), jnp.bfloat16),
-            pltpu.VMEM((f_tiles, tile, 2 * tile), jnp.bfloat16),
             pltpu.VMEM((f_tiles, 2 * tile, tile), jnp.float32),
             pltpu.VMEM((AXES, CUBE, unit, f_tiles * tile), jnp.bfloat16),
             pltpu.VMEM((f_tiles, slots + 1, tile, 2 * tile), jnp.float32),
@@ -406,10 +410,14 @@
             pltpu.VMEM((AXES, 8, unit, 4 * tile), jnp.bfloat16),
             pltpu.VMEM((AXES, 7, unit, 4 * tile), jnp.bfloat16),
             pltpu.VMEM((AXES, 15, unit, 4 * tile), jnp.bfloat16),
+            pltpu.SMEM((f_tiles, slots), jnp.int32),
+            pltpu.SMEM((f_tiles,), jnp.int32),
+            pltpu.SMEM((2, f_tiles), jnp.int32),
             pltpu.SMEM((CUBE + 2, 8, tile), jnp.int32),
-            pltpu.SMEM((4, f_tiles * slots), jnp.int32),
+            pltpu.SMEM((5, f_tiles * slots), jnp.int32),
             pltpu.SMEM((f_tiles * slots,), jnp.int32),
             pltpu.SMEM((f_tiles * 8,), jnp.int32),
+            dma((3,)),
             dma,
             dma,
             dma,

time: 74.1 us -> 74.5 us (level)
  no operation moved by 1% of the time
where the time goes in v4:
time: 74.5 us; the launch traced here: 74.3 us
  Pallas kernels  72.5 us (97%)
  local copies, waits for them, and re-layouts  1.77 us (2%)
    pallas_call x1, Pallas kernels, local(): pl.pallas_call(kernel, out_shape=jax.ShapeDtypeStruct((unit, 24 * tile),...  72.5 us
    unnamed x1, local copies, waits for them, and re-layouts  1.77 us

profile of v4, /device:TPU:8, one launch (start us, length us, event | category | flops | bytes accessed | tf_op | source)
XLA Modules:
  0.0 74.3 jit_solution(15771983926055516577)
XLA Ops:
  0.0 72.5 %shard_map.55 = bf16[64,3072]{1,0:T(8,128)(2,1)} custom-call(bf16[4,10,128,128]{3,2,1,0:T(8,128)(2,1)} %a_hbm.1, s32[4,10]{1,0:T(4,128)} %cols_hbm.1, s32[4]{0:T(128)} %count_hbm.1, bf16[4,128,256]{2,1,0:T(8,128)(2,1)} %p_hbm.1, s32[2,4]{1,0:T(2,128)} %bitcast.1), custom_call_target="tpu_custom_call" | custom-call | tf_op jit(solution)/shard_map/pallas_call | solution.py:396
  72.6 1.8 %copy.7 = bf16[64,3072]{1,0:T(8,128)(2,1)} copy(bf16[64,3072]{1,0:T(8,128)(2,1)} %shard_map.55) | data formatting | bytes 786432

commit v5 on v3

--- a/solution.py
+++ b/solution.py
@@ -10,7 +10,7 @@
 AXES = 4
 CUBE = 16
 LEFT, RIGHT = CUBE, CUBE + 1
-GATHER = [(0, 0), (0, 1), (0, 2), (1, 1), (0, 3), (1, 2), (2, 2), (3, 2), (1, 3), (2, 3), (3, 3),
+GATHER = [(0, 0), (0, 1), (0, 2), (0, 3), (1, 1), (1, 2), (2, 2), (3, 2), (1, 3), (2, 3), (3, 3),
           (4, 3), (5, 3), (6, 3), (7, 3)]
 GATHER_DEPTH = 3
 BASE = [0, 8, 12, 14]

time: 74.1 us -> 74 us (level)
  no operation moved by 1% of the time
where the time goes in v5:
time: 74 us; the launch traced here: 73.8 us
  Pallas kernels  72 us (97%)
  local copies, waits for them, and re-layouts  1.77 us (2%)
    pallas_call x1, Pallas kernels, local(): pl.pallas_call(kernel, out_shape=jax.ShapeDtypeStruct((unit, 24 * tile),...  72 us
    unnamed x1, local copies, waits for them, and re-layouts  1.77 us

profile of v5, /device:TPU:8, one launch (start us, length us, event | category | flops | bytes accessed | tf_op | source)
XLA Modules:
  0.0 73.8 jit_solution(10528382960421110399)
XLA Ops:
  0.0 72.0 %shard_map.55 = bf16[64,3072]{1,0:T(8,128)(2,1)} custom-call(bf16[4,10,128,128]{3,2,1,0:T(8,128)(2,1)} %a_hbm.1, s32[4,10]{1,0:T(4,128)} %cols.1, s32[4]{0:T(128)} %count.1, bf16[4,128,256]{2,1,0:T(8,128)(2,1)} %p_hbm.1, s32[2,4]{1,0:T(2,128)} %bitcast.1), custom_call_target="tpu_custom_call" | custom-call | tf_op jit(solution)/shard_map/pallas_call | solution.py:391
  72.0 1.8 %copy.7 = bf16[64,3072]{1,0:T(8,128)(2,1)} copy(bf16[64,3072]{1,0:T(8,128)(2,1)} %shard_map.55) | data formatting | bytes 786432
